TPU v7x, 256 devices: a whole 4x4x8 slice. The times are simulated.
256 devices in a mesh: snap: 16 (over z, core), vtx: 16 (over y, x).
Axes of the slice: x: 4, y: 4, z: 8, core: 2. Of those that a mesh axis runs over, the one named last changes fastest.
Arguments:
- feats: float32 [16, 16384, 512], P('snap', 'vtx'), may hold values from -6 to 6
- col_ids: int32 [16, 128, 16], P('snap', 'vtx'), may hold values from 0 to 127
- tiles: float32 [16, 128, 16, 128, 128], P('snap', 'vtx'), may hold values from -0.125 to 0.125
- w_first: float32 [512, 256], replicated, may hold values from -0.25 to 0.25
- w_input: float32 [256, 1024], replicated, may hold values from -0.375 to 0.375
- w_recur: float32 [256, 1024], replicated, may hold values from -0.375 to 0.375
- lstm_bias: float32 [1024], replicated, may hold values from -3 to 3
- w_second: float32 [256, 256], replicated, may hold values from -0.375 to 0.375
Outputs:
- output: float32 [16, 16384, 256], P('snap', 'vtx')
Inputs may be any that keep to these rules, and one draw needn't show every extreme that they name: `col_ids`: every entry names a row block of the same snapshot's graph; a few blocks are named far more often than others.
All inputs are finite; a program needn't handle non-finite values.
Results may differ from a plain program's by a relative error of at most 0.0003.
Values sent between devices are 32-bit elements; how exact they have to be, the bound alone decides.
A program may use at most 128 MiB of HBM per device.

v0:
```python
import jax
import jax.numpy as jnp
from jax import lax
from jax.sharding import PartitionSpec as P


def block_sum(tile_set, column_ids, source):
    tile_edge = tile_set.shape[-1]
    width = source.shape[-1]
    blocks = source.reshape(source.shape[0] // tile_edge, tile_edge, width)

    def row_block(operands):
        tiles_here, ids_here = operands
        picked = blocks[ids_here]
        return jnp.einsum("ktu,kuw->tw", tiles_here, picked, precision=lax.Precision.HIGHEST)

    summed = lax.map(row_block, (tile_set, column_ids))
    return summed.reshape(-1, width)


def row_scale(tiles):
    sums = jnp.sum(tiles * tiles, axis=(2, 4))
    return lax.rsqrt(1.0 + sums).reshape(tiles.shape[0], -1)[..., None]


def recurrence(pre_time, w_recur, lstm_bias):
    hidden_size = w_recur.shape[0]

    def advance(carry, pre_step):
        state_h, state_c = carry
        gates = pre_step + jnp.dot(state_h, w_recur, precision=lax.Precision.HIGHEST) + lstm_bias
        gate_i = gates[:, :hidden_size]
        gate_f = gates[:, hidden_size : 2 * hidden_size]
        gate_g = gates[:, 2 * hidden_size : 3 * hidden_size]
        gate_o = gates[:, 3 * hidden_size :]
        state_c = jax.nn.sigmoid(gate_f) * state_c + jax.nn.sigmoid(gate_i) * jnp.tanh(gate_g)
        state_h = jax.nn.sigmoid(gate_o) * jnp.tanh(state_c)
        return ((state_h, state_c), state_h)

    zeros = jnp.zeros((pre_time.shape[1], hidden_size), jnp.float32)
    _, states = lax.scan(advance, (zeros, zeros), pre_time)
    return states


def on_device(feats, col_ids, tiles, w_first, w_input, w_recur, lstm_bias, w_second):
    scale = row_scale(tiles)
    whole = lax.all_gather(feats, "vtx", axis=1, tiled=True)
    mixed = scale * (feats + jax.vmap(block_sum)(tiles, col_ids, whole))
    hidden_one = jax.nn.relu(
        jnp.einsum("svf,fh->svh", mixed, w_first, precision=lax.Precision.HIGHEST)
    )
    timelines = lax.all_to_all(hidden_one, "snap", split_axis=1, concat_axis=0, tiled=True)
    pre_time = jnp.einsum("svh,hg->svg", timelines, w_input, precision=lax.Precision.HIGHEST)
    states = recurrence(pre_time, w_recur, lstm_bias)
    returned = lax.all_to_all(states, "snap", split_axis=0, concat_axis=1, tiled=True)
    whole_two = lax.all_gather(returned, "vtx", axis=1, tiled=True)
    mixed_two = scale * (returned + jax.vmap(block_sum)(tiles, col_ids, whole_two))
    return jnp.einsum("svh,hg->svg", mixed_two, w_second, precision=lax.Precision.HIGHEST)


def solution(mesh):
    placed = (
        P("snap", "vtx", None),
        P("snap", "vtx", None),
        P("snap", "vtx", None, None, None),
        P(),
        P(),
        P(),
        P(),
        P(),
    )
    return jax.shard_map(
        on_device, mesh=mesh, in_specs=placed, out_specs=P("snap", "vtx", None), check_vma=False
    )
```

profile of v0, /device:TPU:1, one launch (start us, length us, event | category | flops | bytes accessed | tf_op | source)
XLA Modules:
  0.0 617.5 jit_solution(13330983946178340313)
XLA Ops:
  11.3 204.4 %all-gather.3.cloned.1.call-done = f32[1,16384,512]{2,1,0:T(8,128)} async-done(((f32[1,1024,512]{2,1,0:T(8,128)}), f32[1,16384,512]{2,1,0:T(8,128)}) %all-gather.3.cloned.1.call-update) | async-done | bytes 33554448 | tf_op jit(solution)/shard_map/all_gather | solution.py:47
  215.7 91.2 %while.35 = (s32[]{:T(128)}, f32[8,1,128,512]{3,2,1,0:T(8,128)}, f32[8,1,16,128,128]{4,3,2,1,0:T(8,128)}, s32[8,1,16]{2,1,0:T(1,128)}, f32[1,128,128,512]{3,2,1,0:T(8,128)}, /*index=5*/s32[]{:T(128)}) while((s32[]{:T(128)}, f32[8,1,128,512]{3,2,1,0:T(8,128)}, f32[8,1,16,128,128]{4,3,2,1,0:T(8,128)}, s32[8,1,16]{2,1,0:T(1,128)}, ...), condition=%wide.region_2.3_spmd, body=%wide.region_1.2_spmd.sunk | while | flops 1610612864 | bytes 13895369 | solution.py:17
  221.6 5.7 fusion.62
  232.9 5.7 fusion.62
  244.3 5.7 fusion.62
  255.7 5.7 fusion.62
  267.2 5.6 fusion.62
  278.6 5.6 fusion.62
  289.9 5.6 fusion.62
  301.2 5.7 fusion.62
  312.5 7.8 %all-to-all-start = ((f32[1,1024,256]{2,0,1:T(1,128)}), f32[1,1024,256]{2,0,1:T(1,128)S(1)}, u32[]{:S(2)}, u32[]{:S(2)}) async-start(f32[1,1024,256]{2,0,1:T(1,128)} %copy.12), calls=%async_computation | async-start | bytes 2097152 | tf_op jit(solution)/shard_map/all_to_all | solution.py:52
  320.4 27.9 %all-to-all-done = f32[1,1024,256]{2,0,1:T(1,128)S(1)} async-done(((f32[1,1024,256]{2,0,1:T(1,128)}), f32[1,1024,256]{2,0,1:T(1,128)S(1)}, u32[]{:S(2)}, u32[]{:S(2)}) %all-to-all-start) | async-done | bytes 1048608 | tf_op jit(solution)/shard_map/all_to_all | solution.py:52
  353.3 29.0 %while.37 = (s32[]{:T(128)}, f32[64,256]{1,0:T(8,128)S(1)}, f32[64,256]{1,0:T(8,128)S(1)}, f32[16,64,256]{2,1,0:T(8,128)S(1)}, f32[16,64,1024]{2,1,0:T(8,128)}, ...) while((s32[]{:T(128)}, f32[64,256]{1,0:T(8,128)S(1)}, ...), condition=%wide.region_4.5_spmd.clone, body=%wide.region_3.4_spmd.clone.sunk | while | flops 201703424 | bytes 2166896 | solution.py:41
  382.4 32.0 %all_to_all.27 = f32[16,64,256]{2,1,0:T(8,128)} all-to-all(f32[16,64,256]{2,1,0:T(8,128)S(1)} %get-tuple-element.97), channel_id=1, replica_groups=mesh['snap'=16,'vtx'=16] {'snap'}, dimensions={0} | all-to-all | bytes 2097152 | tf_op jit(solution)/shard_map/all_to_all | solution.py:55
  414.4 111.3 %all-gather.5.cloned.1.call-done = f32[1,16384,256]{2,1,0:T(8,128)} async-done(((f32[1,1024,256]{2,1,0:T(8,128)}), f32[1,16384,256]{2,1,0:T(8,128)}) %all-gather.5.cloned.1.call-update) | async-done | bytes 16777232 | tf_op jit(solution)/shard_map/all_gather | solution.py:56
  525.7 81.2 %while.36 = (s32[]{:T(128)}, f32[8,1,128,256]{3,2,1,0:T(8,128)}, f32[8,1,16,128,128]{4,3,2,1,0:T(8,128)}, s32[8,1,16]{2,1,0:T(1,128)}, f32[1,128,128,256]{3,2,1,0:T(8,128)}, /*index=5*/s32[]{:T(128)}) while((s32[]{:T(128)}, f32[8,1,128,256]{3,2,1,0:T(8,128)}, f32[8,1,16,128,128]{4,3,2,1,0:T(8,128)}, s32[8,1,16]{2,1,0:T(1,128)}, ...), condition=%wide.region_6.7_spmd, body=%wide.region_5.6_spmd.sunk | while | flops 805306496 | bytes 7472841 | solution.py:17
  526.4 6.4 %gather_fusion.1 = f32[16,128,256]{2,1,0:T(8,128)S(1)} fusion(f32[1,128,128,256]{3,2,1,0:T(8,128)} %get-tuple-element.352, s32[16]{0:T(128)S(1)} %or_bitcast_fusion.5), kind=kCustom, calls=%fused_computation.1.clone.1 | custom fusion | bytes 4194432 | tf_op jit(solution)/shard_map/vmap()/while/body/eval_jaxpr/gather | solution.py:14
  536.5 6.4 %gather_fusion.1 = f32[16,128,256]{2,1,0:T(8,128)S(1)} fusion(f32[1,128,128,256]{3,2,1,0:T(8,128)} %get-tuple-element.352, s32[16]{0:T(128)S(1)} %or_bitcast_fusion.5), kind=kCustom, calls=%fused_computation.1.clone.1 | custom fusion | bytes 4194432 | tf_op jit(solution)/shard_map/vmap()/while/body/eval_jaxpr/gather | solution.py:14
  546.7 6.4 %gather_fusion.1 = f32[16,128,256]{2,1,0:T(8,128)S(1)} fusion(f32[1,128,128,256]{3,2,1,0:T(8,128)} %get-tuple-element.352, s32[16]{0:T(128)S(1)} %or_bitcast_fusion.5), kind=kCustom, calls=%fused_computation.1.clone.1 | custom fusion | bytes 4194432 | tf_op jit(solution)/shard_map/vmap()/while/body/eval_jaxpr/gather | solution.py:14
  556.8 6.4 %gather_fusion.1 = f32[16,128,256]{2,1,0:T(8,128)S(1)} fusion(f32[1,128,128,256]{3,2,1,0:T(8,128)} %get-tuple-element.352, s32[16]{0:T(128)S(1)} %or_bitcast_fusion.5), kind=kCustom, calls=%fused_computation.1.clone.1 | custom fusion | bytes 4194432 | tf_op jit(solution)/shard_map/vmap()/while/body/eval_jaxpr/gather | solution.py:14
  567.0 6.4 %gather_fusion.1 = f32[16,128,256]{2,1,0:T(8,128)S(1)} fusion(f32[1,128,128,256]{3,2,1,0:T(8,128)} %get-tuple-element.352, s32[16]{0:T(128)S(1)} %or_bitcast_fusion.5), kind=kCustom, calls=%fused_computation.1.clone.1 | custom fusion | bytes 4194432 | tf_op jit(solution)/shard_map/vmap()/while/body/eval_jaxpr/gather | solution.py:14
  577.1 6.4 %gather_fusion.1 = f32[16,128,256]{2,1,0:T(8,128)S(1)} fusion(f32[1,128,128,256]{3,2,1,0:T(8,128)} %get-tuple-element.352, s32[16]{0:T(128)S(1)} %or_bitcast_fusion.5), kind=kCustom, calls=%fused_computation.1.clone.1 | custom fusion | bytes 4194432 | tf_op jit(solution)/shard_map/vmap()/while/body/eval_jaxpr/gather | solution.py:14
  587.3 6.4 %gather_fusion.1 = f32[16,128,256]{2,1,0:T(8,128)S(1)} fusion(f32[1,128,128,256]{3,2,1,0:T(8,128)} %get-tuple-element.352, s32[16]{0:T(128)S(1)} %or_bitcast_fusion.5), kind=kCustom, calls=%fused_computation.1.clone.1 | custom fusion | bytes 4194432 | tf_op jit(solution)/shard_map/vmap()/while/body/eval_jaxpr/gather | solution.py:14
  597.4 6.4 %gather_fusion.1 = f32[16,128,256]{2,1,0:T(8,128)S(1)} fusion(f32[1,128,128,256]{3,2,1,0:T(8,128)} %get-tuple-element.352, s32[16]{0:T(128)S(1)} %or_bitcast_fusion.5), kind=kCustom, calls=%fused_computation.1.clone.1 | custom fusion | bytes 4194432 | tf_op jit(solution)/shard_map/vmap()/while/body/eval_jaxpr/gather | solution.py:14
  (123 shorter events, 123.3 us)
Async XLA Ops:
  6.5 341.8 %copy-start = (f32[256,1024]{1,0:T(8,128)S(1)}, f32[256,1024]{1,0:T(8,128)}, u32[]{:S(2)}) copy-start(f32[256,1024]{1,0:T(8,128)} %param.18) | copy-start | bytes 3145732
  6.5 209.2 %all-gather.3.cloned.1.call-start = ((), (), s32[]{:S(2)}) async-start(), calls=%async_computation.2 | async-start | bytes 35651584 | tf_op jit(solution)/shard_map/all_gather | solution.py:47
  215.7 91.2 %copy-start.2 = (f32[1,1024,512]{2,1,0:T(8,128)S(1)}, f32[1,1024,512]{2,1,0:T(8,128)}, u32[]{:S(2)}) copy-start(f32[1,1024,512]{2,1,0:T(8,128)} %param.14) | copy-start | bytes 6291460
  312.5 35.7 %all-to-all-start = ((f32[1,1024,256]{2,0,1:T(1,128)}), f32[1,1024,256]{2,0,1:T(1,128)S(1)}, u32[]{:S(2)}, u32[]{:S(2)}) async-start(f32[1,1024,256]{2,0,1:T(1,128)} %copy.12), calls=%async_computation | async-start | bytes 2097152 | tf_op jit(solution)/shard_map/all_to_all | solution.py:52
  320.3 205.4 %all-gather.5.cloned.1.call-start = ((), (), s32[]{:S(2)}) async-start(), calls=%async_computation.3 | async-start | bytes 17825792 | tf_op jit(solution)/shard_map/all_gather | solution.py:56
  348.3 5.0 copy-start.1
  348.3 5.0 copy-start.4
  606.9 1.8 copy-start.3
Sparse Core Ops, SparseCore 0:
  9.8 205.8 all-gather.2
  414.5 111.1 all-gather.4
where the time goes:
time: 619 us; the launch traced here: 617 us
  waiting for transfers between devices  344 us (56%)
  matrix products  107 us (17%)
  local copies, waits for them, and re-layouts  94.3 us (15%)
  blocking collectives  32 us (5%)
  other arithmetic  18 us (3%)
  between operations  13.5 us (2%)
  starting transfers between devices  7.85 us (1%)
    all_gather x1, waiting for transfers between devices, on_device(): whole = lax.all_gather(feats, 'vtx', axis=1, tiled=True)  204 us
    all_gather x1, waiting for transfers between devices, on_device(): whole_two = lax.all_gather(returned, 'vtx', axis=1, tiled=True)  111 us
    gather x32, local copies, waits for them, and re-layouts, row_block(): picked = blocks[ids_here]  92.1 us
    dot_general x16, matrix products, row_block(): jnp.einsum('ktu,kuw->tw', tiles_here, picked, precision=lax.Precision.HIG...  69.3 us
    all_to_all x1, blocking collectives, on_device(): lax.all_to_all(states, 'snap', split_axis=0, concat_axis=1, tiled=True)  32 us
    all_to_all x1, waiting for transfers between devices, on_device(): lax.all_to_all(hidden_one, 'snap', split_axis=1, concat_axis=0, tiled=True)  27.9 us
    dot_general x16, matrix products, advance(): jnp.dot(state_h, w_recur, precision=lax.Precision.HIGHEST)  27.3 us
  transfers between devices with their start and end apart: 3, of which 3 were waited for; matrix products, arithmetic and copies ran while one was open for 1% of the time, Pallas kernels for 0%

commit v1 on v0

--- a/solution.py
+++ b/solution.py
@@ -2,6 +2,14 @@
 import jax.numpy as jnp
 from jax import lax
 from jax.sharding import PartitionSpec as P
+
+
+def follow_the_threads(original, row_dim):
+    state_next = jnp.stack(lax.axis_size("vtx") * [original], axis=0)
+    raw_out = jnp.concatenate(
+        lax.all_to_all(state_next, axis_name="vtx", split_axis=0, concat_axis=0), row_dim
+    )
+    return raw_out
 
 
 def block_sum(tile_set, column_ids, source):
@@ -44,7 +52,7 @@
 
 def on_device(feats, col_ids, tiles, w_first, w_input, w_recur, lstm_bias, w_second):
     scale = row_scale(tiles)
-    whole = lax.all_gather(feats, "vtx", axis=1, tiled=True)
+    whole = follow_the_threads(feats, 1)
     mixed = scale * (feats + jax.vmap(block_sum)(tiles, col_ids, whole))
     hidden_one = jax.nn.relu(
         jnp.einsum("svf,fh->svh", mixed, w_first, precision=lax.Precision.HIGHEST)

time: 619 us -> 932 us (1.51)
  waiting for transfers between devices: 344 us -> 631 us
  starting transfers between devices: 7.85 us -> 20.9 us
  local copies, waits for them, and re-layouts: 94.3 us -> 106 us
    all_to_all x0 -> x1, waiting for transfers between devices: none -> 494 us  [follow_the_threads(): lax.all_to_all(state_next, axis_name='vtx', split_axis=0, concat_axis=0)]
    all_gather x1 -> x0, waiting for transfers between devices: 204 us -> none  [on_device(): whole = lax.all_gather(feats, 'vtx', axis=1, tiled=True)]
    another operation x0 -> x1, local copies, waits for them, and re-layouts: none -> 12.3 us  [follow_the_threads(): state_next = jnp.stack(lax.axis_size('vtx') * [original], axis=0)]
  transfers between devices with their start and end apart: 3 -> 3, of which waited for: 3 -> 3; matrix products, arithmetic and copies ran while one was open for 1% -> 0% of each run, Pallas kernels for 0% -> 0%
where the time goes in v1:
time: 932 us; the launch traced here: 930 us
  waiting for transfers between devices  631 us (68%)
  matrix products  107 us (11%)
  local copies, waits for them, and re-layouts  106 us (11%)
  blocking collectives  32 us (3%)
  starting transfers between devices  20.9 us (2%)
  other arithmetic  18 us (2%)
  between operations  13.5 us (1%)
    all_to_all x1, waiting for transfers between devices, follow_the_threads(): lax.all_to_all(state_next, axis_name='vtx', split_axis=0, concat_axis=0)  494 us
    all_gather x1, waiting for transfers between devices, on_device(): whole_two = lax.all_gather(returned, 'vtx', axis=1, tiled=True)  109 us
    gather x32, local copies, waits for them, and re-layouts, row_block(): picked = blocks[ids_here]  92.1 us
    dot_general x16, matrix products, row_block(): jnp.einsum('ktu,kuw->tw', tiles_here, picked, precision=lax.Precision.HIG...  69.4 us
    all_to_all x1, blocking collectives, on_device(): lax.all_to_all(states, 'snap', split_axis=0, concat_axis=1, tiled=True)  32 us
    all_to_all x1, waiting for transfers between devices, on_device(): lax.all_to_all(hidden_one, 'snap', split_axis=1, concat_axis=0, tiled=True)  27.9 us
    dot_general x16, matrix products, advance(): jnp.dot(state_h, w_recur, precision=lax.Precision.HIGHEST)  27.3 us
  transfers between devices with their start and end apart: 3, of which 3 were waited for; matrix products, arithmetic and copies ran while one was open for 0% of the time, Pallas kernels for 0%

profile of v1, /device:TPU:1, one launch (start us, length us, event | category | flops | bytes accessed | tf_op | source)
XLA Modules:
  0.0 929.7 jit_solution(15968206536600326492)
XLA Ops:
  6.5 12.3 %stack.2 = f32[16,1,1024,512]{3,2,1,0:T(8,128)} broadcast(f32[1024,512]{1,0:T(8,128)} %bitcast.110), dimensions={2,3} | broadcast | bytes 35651584 | tf_op jit(solution)/shard_map/stack | solution.py:8
  18.8 7.6 all-to-all-start
  30.5 493.9 %all-to-all-done = f32[16,1,1024,512]{3,2,1,0:T(8,128)} async-done(((f32[16,1,1024,512]{3,2,1,0:T(8,128)}), f32[16,1,1024,512]{3,2,1,0:T(8,128)}, u32[]{:S(2)}, u32[]{:S(2)}) %all-to-all-start) | async-done | bytes 33554464 | tf_op jit(solution)/shard_map/all_to_all | solution.py:10
  524.4 91.2 %while.35 = (s32[]{:T(128)}, f32[8,1,128,512]{3,2,1,0:T(8,128)}, f32[8,1,16,128,128]{4,3,2,1,0:T(8,128)}, s32[8,1,16]{2,1,0:T(1,128)}, f32[1,128,128,512]{3,2,1,0:T(8,128)}, /*index=5*/s32[]{:T(128)}) while((s32[]{:T(128)}, f32[8,1,128,512]{3,2,1,0:T(8,128)}, f32[8,1,16,128,128]{4,3,2,1,0:T(8,128)}, s32[8,1,16]{2,1,0:T(1,128)}, ...), condition=%wide.region_2.3_spmd, body=%wide.region_1.2_spmd.sunk | while | flops 1610612864 | bytes 13895369 | solution.py:25
  530.2 5.7 fusion.62
  552.9 5.7 fusion.62
  564.3 5.7 fusion.62
  575.7 5.7 fusion.62
  587.2 5.7 fusion.62
  598.5 5.7 fusion.62
  621.1 13.2 %all-to-all-start.1 = ((f32[1,1024,256]{2,0,1:T(1,128)}), f32[1,1024,256]{2,0,1:T(1,128)S(1)}, u32[]{:S(2)}, u32[]{:S(2)}) async-start(f32[1,1024,256]{2,0,1:T(1,128)} %copy.12), calls=%async_computation.1 | async-start | bytes 2097152 | tf_op jit(solution)/shard_map/all_to_all | solution.py:60
  634.4 27.9 %all-to-all-done.1 = f32[1,1024,256]{2,0,1:T(1,128)S(1)} async-done(((f32[1,1024,256]{2,0,1:T(1,128)}), f32[1,1024,256]{2,0,1:T(1,128)S(1)}, u32[]{:S(2)}, u32[]{:S(2)}) %all-to-all-start.1) | async-done | bytes 1048608 | tf_op jit(solution)/shard_map/all_to_all | solution.py:60
  667.4 29.0 %while.37 = (s32[]{:T(128)}, f32[64,256]{1,0:T(8,128)S(1)}, f32[64,256]{1,0:T(8,128)S(1)}, f32[16,64,256]{2,1,0:T(8,128)S(1)}, f32[16,64,1024]{2,1,0:T(8,128)}, ...) while((s32[]{:T(128)}, f32[64,256]{1,0:T(8,128)S(1)}, ...), condition=%wide.region_4.5_spmd.clone, body=%wide.region_3.4_spmd.clone.sunk | while | flops 201703424 | bytes 2166896 | solution.py:49
  696.5 32.0 %all_to_all.32 = f32[16,64,256]{2,1,0:T(8,128)} all-to-all(f32[16,64,256]{2,1,0:T(8,128)S(1)} %get-tuple-element.97), channel_id=1, replica_groups=mesh['snap'=16,'vtx'=16] {'snap'}, dimensions={0} | all-to-all | bytes 2097152 | tf_op jit(solution)/shard_map/all_to_all | solution.py:63
  728.5 109.4 %all-gather.2.cloned.1.call-done = f32[1,16384,256]{2,1,0:T(8,128)} async-done(((f32[1,1024,256]{2,1,0:T(8,128)}), f32[1,16384,256]{2,1,0:T(8,128)}) %all-gather.2.cloned.1.call-update) | async-done | bytes 16777232 | tf_op jit(solution)/shard_map/all_gather | solution.py:64
  837.9 81.2 %while.36 = (s32[]{:T(128)}, f32[8,1,128,256]{3,2,1,0:T(8,128)}, f32[8,1,16,128,128]{4,3,2,1,0:T(8,128)}, s32[8,1,16]{2,1,0:T(1,128)}, f32[1,128,128,256]{3,2,1,0:T(8,128)}, /*index=5*/s32[]{:T(128)}) while((s32[]{:T(128)}, f32[8,1,128,256]{3,2,1,0:T(8,128)}, f32[8,1,16,128,128]{4,3,2,1,0:T(8,128)}, s32[8,1,16]{2,1,0:T(1,128)}, ...), condition=%wide.region_6.7_spmd, body=%wide.region_5.6_spmd.sunk | while | flops 805306496 | bytes 7472841 | solution.py:25
  838.6 6.4 gather_fusion.1
  848.7 6.4 gather_fusion.1
  858.9 6.4 gather_fusion.1
  869.0 6.4 gather_fusion.1
  879.2 6.4 gather_fusion.1
  889.3 6.4 gather_fusion.1
  899.5 6.4 gather_fusion.1
  909.6 6.4 gather_fusion.1
  (123 shorter events, 133.9 us)
Async XLA Ops:
  6.5 655.8 %copy-start = (f32[256,1024]{1,0:T(8,128)S(1)}, f32[256,1024]{1,0:T(8,128)}, u32[]{:S(2)}) copy-start(f32[256,1024]{1,0:T(8,128)} %param.18) | copy-start | bytes 3145732
  18.8 505.5 %all-to-all-start = ((f32[16,1,1024,512]{3,2,1,0:T(8,128)}), f32[16,1,1024,512]{3,2,1,0:T(8,128)}, u32[]{:S(2)}, u32[]{:S(2)}) async-start(f32[16,1,1024,512]{3,2,1,0:T(8,128)} %stack.2), calls=%async_computation | async-start | bytes 67108864 | tf_op jit(solution)/shard_map/all_to_all | solution.py:10
  524.4 91.2 %copy-start.2 = (f32[1,1024,512]{2,1,0:T(8,128)S(1)}, f32[1,1024,512]{2,1,0:T(8,128)}, u32[]{:S(2)}) copy-start(f32[1,1024,512]{2,1,0:T(8,128)} %param.14) | copy-start | bytes 6291460
  621.1 41.2 %all-to-all-start.1 = ((f32[1,1024,256]{2,0,1:T(1,128)}), f32[1,1024,256]{2,0,1:T(1,128)S(1)}, u32[]{:S(2)}, u32[]{:S(2)}) async-start(f32[1,1024,256]{2,0,1:T(1,128)} %copy.12), calls=%async_computation.1 | async-start | bytes 2097152 | tf_op jit(solution)/shard_map/all_to_all | solution.py:60
  634.4 203.5 %all-gather.2.cloned.1.call-start = ((), (), s32[]{:S(2)}) async-start(), calls=%async_computation.3 | async-start | bytes 17825792 | tf_op jit(solution)/shard_map/all_gather | solution.py:64
  662.4 5.1 copy-start.1
  662.4 5.0 copy-start.4
  919.1 1.8 copy-start.3
Sparse Core Ops, SparseCore 0:
  728.6 109.2 all-gather.1
